TPU v7x, 32 devices: a whole 2x2x4 slice. The times are simulated.
32 devices in a mesh: patch: 2 (over x), sim: 16 (over z, y, core).
Axes of the slice: x: 2, y: 2, z: 4, core: 2. Of those that a mesh axis runs over, the one named last changes fastest.
Arguments:
- sky_maps: bfloat16 [2048, 2048], P(('patch', 'sim')), parts along dimension 0, may hold values from -6 to 6
- ivf_maps: bfloat16 [2048, 2048], P(('patch', 'sim')), parts along dimension 0, may hold values from -6 to 6
- sim_sky: bfloat16 [8, 2048, 2048], P(None, ('patch', 'sim')), parts along dimension 1, may hold values from -6 to 6
- sim_ivf: bfloat16 [8, 2048, 2048], P(None, ('patch', 'sim')), parts along dimension 1, may hold values from -6 to 6
- ra_wiener: bfloat16 [1024, 1024], replicated, may hold values from -0.1875 to 0.1875
- ra_gradient: bfloat16 [1024, 1024], replicated, may hold values from -0.1875 to 0.1875
- pair_table: int32 [8, 8], replicated, may hold values 0 or 1
- sim_index: int32 [4], replicated, may hold values from 0 to 7
- source_pixels: int32 [8192], P('patch'), parts along dimension 0, may hold values from 0 to 262143
- response: float32 [256], P('patch'), parts along dimension 0, may hold values from 0.2 to 2
Outputs:
- lens_split: float32 [2048, 2048], P(('patch', 'sim')), parts along dimension 0
There are 2 independent parts, one for each index of `patch`. A program takes and returns all parts, laid end to end along the dimension named above; an argument that names none is the same for every part. Nothing has to cross between parts.
Inputs may be any that keep to these rules, and one draw needn't show every extreme that they name: `sim_index`: indices into the cached evolutions; entries may repeat. `source_pixels`: flat pixel indices of the patch; entries may repeat.
All inputs are finite; a program needn't handle non-finite values.
Results may differ from a plain program's by a relative error of at most 0.0035.
Values may be sent and summed in bfloat16 or wider, within the bound.
No kernel may reach another device: no remote copies, remote signals or barrier semaphores. Data moves between devices by JAX's collectives and lax.ppermute only.
A program may use at most 128 MiB of HBM per device.

v0:
```python
import jax
import jax.numpy as jnp
from jax import lax
from jax.sharding import PartitionSpec as P

NSPLIT = 8
NUSE = 4


def extended(cells, sides, width):
    for axis, dim in sides:
        count = lax.axis_size(axis)
        head = lax.slice_in_dim(cells, 0, width, axis=dim)
        tail = lax.slice_in_dim(cells, cells.shape[dim] - width, cells.shape[dim], axis=dim)
        cells = jnp.concatenate(
            [
                lax.ppermute(tail, axis, [(i, (i + 1) % count) for i in range(count)]),
                cells,
                lax.ppermute(head, axis, [((i + 1) % count, i) for i in range(count)]),
            ],
            axis=dim,
        )
    return cells


def from_behind(block, axis, distance):
    devices = range(lax.axis_size(axis))
    route = [((i - distance) % len(devices), i) for i in devices]
    return lax.ppermute(block, axis, route)


def tile_apply(values, matrix):
    width = matrix.shape[0]
    shaped = values.reshape(values.shape[:-1] + (values.shape[-1] // width, width))
    result = jnp.einsum("...tc,cd->...td", shaped, matrix, preferred_element_type=jnp.float32)
    return result.reshape(values.shape)


def trim_edges(padded, band_index, group_bands):
    lower_keep = (band_index > 0).astype(padded.dtype)
    upper_keep = (band_index < group_bands - 1).astype(padded.dtype)
    return jnp.concatenate(
        [padded[:, :1] * lower_keep, padded[:, 1:-1], padded[:, -1:] * upper_keep], axis=1
    )


def row_slope(padded):
    upper = padded[:, 2:].astype(jnp.float32)
    lower = padded[:, :-2].astype(jnp.float32)
    return (upper - lower) * 0.5


def on_device(
    sky_maps,
    ivf_maps,
    sim_sky,
    sim_ivf,
    ra_wiener,
    ra_gradient,
    pair_table,
    sim_index,
    source_pixels,
    response,
):
    axis_count = lax.axis_size("sim")
    group_bands = axis_count // NSPLIT
    device_index = lax.axis_index("sim")
    logical = (device_index - group_bands // 2) % axis_count
    band_index = logical % group_bands
    split_index = logical // group_bands
    rows = sky_maps.shape[0]
    columns = sky_maps.shape[1]
    chosen_sky = jnp.concatenate([sky_maps[None], jnp.take(sim_sky, sim_index, axis=0)], axis=0)
    chosen_ivf = jnp.concatenate([ivf_maps[None], jnp.take(sim_ivf, sim_index, axis=0)], axis=0)
    offsets = source_pixels - band_index * rows * columns
    inside = (offsets >= 0) & (offsets < rows * columns)
    offsets = jnp.where(inside, offsets, rows * columns)
    hit = jnp.zeros((rows * columns,), jnp.bfloat16).at[offsets].set(1, mode="drop")
    keep = (1 - hit).reshape(rows, columns)
    masked = chosen_ivf * keep[None]
    wiener = tile_apply(chosen_sky, ra_wiener).astype(jnp.bfloat16)
    padded = extended(masked, (("sim", 1),), 1)
    padded = trim_edges(padded, band_index, group_bands)
    pair_row = lax.dynamic_index_in_dim(pair_table, split_index, 0, keepdims=False)
    others = jnp.arange(NSPLIT) != split_index
    weights_row = jnp.where(others, pair_row, 0).astype(jnp.float32)
    empty = jnp.zeros(masked.shape, jnp.float32)
    totals = (empty, empty, empty)
    moving = padded
    for step in range(NSPLIT - 1):
        moving = from_behind(moving, "sim", group_bands)
        factor = weights_row[(split_index - step - 1) % NSPLIT]
        middle = moving[:, 1:-1]
        absorb_total_ra = totals[0] + factor * tile_apply(middle, ra_gradient)
        absorb_total_dec = totals[1] + factor * row_slope(moving)
        absorb_total_src = totals[2] + factor * middle.astype(jnp.float32)
        totals = (absorb_total_ra, absorb_total_dec, absorb_total_src)
    total_ra, total_dec, total_src = totals
    wiener_wide = wiener.astype(jnp.float32)
    flux_ra = (wiener_wide * total_ra).astype(jnp.bfloat16)
    flux_dec = wiener_wide * total_dec
    flux_pad = extended(flux_dec.astype(jnp.bfloat16), (("sim", 1),), 1).astype(flux_dec.dtype)
    flux_pad = trim_edges(flux_pad, band_index, group_bands)
    divergence = tile_apply(flux_ra, ra_gradient) + row_slope(flux_pad)
    weight_rows = lax.dynamic_slice_in_dim(response, band_index * rows, rows)
    hardened = -divergence - weight_rows[None, :, None] * (wiener_wide * total_src)
    return hardened[0] - jnp.sum(hardened[1:], axis=0) / NUSE


def solution(mesh):
    in_specs = (
        P(("patch", "sim"), None),
        P(("patch", "sim"), None),
        P(None, ("patch", "sim"), None),
        P(None, ("patch", "sim"), None),
        P(),
        P(),
        P(),
        P(),
        P("patch"),
        P("patch"),
    )
    out_specs = P(("patch", "sim"), None)
    return jax.shard_map(
        on_device, mesh=mesh, in_specs=in_specs, out_specs=out_specs, check_vma=False
    )
```

profile of v0, /device:TPU:0, one launch (start us, length us, event | category | flops | bytes accessed | tf_op | source)
XLA Modules:
  0.0 324.9 jit_solution(11645422656141791755)
XLA Ops:
  1.5 2.2 gather_fusion.1
  3.7 3.2 gather_fusion
  6.9 28.7 %scatter_custom_fusion = bf16[131072]{0:T(1024)(128)(2,1)S(1)} fusion(s32[4096]{0:T(1024)S(1)} %compare_select_fusion, bf16[4096]{0:T(1024)(128)(2,1)S(1)} %broadcast.54, bf16[]{:T(256)} %constant.125.clone.1), kind=kCustom, calls=%fused_computation.60 | custom fusion | bytes 262146 | tf_op jit(solution)/shard_map/scatter | solution.py:78
  36.3 1.8 mul.218
  38.1 2.5 broadcast_select_fusion
  40.9 5.5 %collective-permute-start.1 = (bf16[5,1,2048]{2,1,0:T(2,128)(2,1)S(1)}, bf16[5,1,2048]{2,1,0:T(2,128)(2,1)}, u32[]{:S(2)}, u32[]{:S(2)}) collective-permute-start(bf16[5,1,2048]{2,1,0:T(2,128)(2,1)S(1)} %get-tuple-element.11), channel_id=1, source_target_pairs={{1,0},{2,1},{3,2},{4,3},{5,4},{6,5},{7,6},{8,7},{9,8},{10,9},{11,1... | collective-permute-start | bytes 61448 | tf_op jit(solution)/shard_map/ppermute | solution.py:19
  46.4 1.7 collective-permute-done.1
  48.9 3.6 %collective-permute-done = bf16[5,1,2048]{2,1,0:T(2,128)(2,1)S(1)} collective-permute-done((bf16[5,1,2048]{2,1,0:T(2,128)(2,1)S(1)}, bf16[5,1,2048]{2,1,0:T(2,128)(2,1)S(1)}, u32[]{:S(2)}, u32[]{:S(2)}) %collective-permute-start) | collective-permute-done | bytes 20512 | tf_op jit(solution)/shard_map/ppermute | solution.py:17
  53.0 33.8 %collective-permute-done.2 = bf16[5,66,2048]{2,1,0:T(8,128)(2,1)S(1)} collective-permute-done((bf16[5,66,2048]{2,1,0:T(8,128)(2,1)S(1)}, bf16[5,66,2048]{2,1,0:T(8,128)(2,1)S(1)}, u32[]{:S(2)}, u32[]{:S(2)}) %collective-permute-start.2) | collective-permute-done | bytes 1351712 | tf_op jit(solution)/shard_map/ppermute | solution.py:29
  88.0 32.9 %collective-permute-done.3 = bf16[5,66,2048]{2,1,0:T(8,128)(2,1)S(1)} collective-permute-done((bf16[5,66,2048]{2,1,0:T(8,128)(2,1)S(1)}, bf16[5,66,2048]{2,1,0:T(8,128)(2,1)S(1)}, u32[]{:S(2)}, u32[]{:S(2)}) %collective-permute-start.3) | collective-permute-done | bytes 1351712 | tf_op jit(solution)/shard_map/ppermute | solution.py:29
  122.0 31.9 %collective-permute-done.4 = bf16[5,66,2048]{2,1,0:T(8,128)(2,1)S(1)} collective-permute-done((bf16[5,66,2048]{2,1,0:T(8,128)(2,1)S(1)}, bf16[5,66,2048]{2,1,0:T(8,128)(2,1)S(1)}, u32[]{:S(2)}, u32[]{:S(2)}) %collective-permute-start.4) | collective-permute-done | bytes 1351712 | tf_op jit(solution)/shard_map/ppermute | solution.py:29
  155.1 32.2 %collective-permute-done.5 = bf16[5,66,2048]{2,1,0:T(8,128)(2,1)} collective-permute-done((bf16[5,66,2048]{2,1,0:T(8,128)(2,1)S(1)}, bf16[5,66,2048]{2,1,0:T(8,128)(2,1)}, u32[]{:S(2)}, u32[]{:S(2)}) %collective-permute-start.5) | collective-permute-done | bytes 1351712 | tf_op jit(solution)/shard_map/ppermute | solution.py:29
  189.6 30.2 %collective-permute-done.6 = bf16[5,66,2048]{2,1,0:T(8,128)(2,1)} collective-permute-done((bf16[5,66,2048]{2,1,0:T(8,128)(2,1)}, bf16[5,66,2048]{2,1,0:T(8,128)(2,1)}, u32[]{:S(2)}, u32[]{:S(2)}) %collective-permute-start.6) | collective-permute-done | bytes 1351712 | tf_op jit(solution)/shard_map/ppermute | solution.py:29
  219.8 3.4 %fusion.29 = bf16[5,64,2,1024]{3,1,2,0:T(8,128)(2,1)S(1)} fusion(bf16[1024,1024]{1,0:T(8,128)(2,1)} %param.16, bf16[4,64,2,1024]{3,1,2,0:T(8,128)(2,1)} %bitcast.97, bf16[1,64,2,1024]{3,1,2,0:T(8,128)(2,1)S(1)} %copy.11), kind=kOutput, calls=%fused_computation.34 | convolution fusion | flops 1343488000 | bytes 4718592 | tf_op jit(solution)/shard_map/...tc,cd->...td/dot_general | solution.py:35
  223.7 1.7 copy.33
  231.3 1.7 slice.136
  233.1 3.1 fusion.22
  236.5 3.0 fusion.20
  239.9 12.4 %collective-permute-done.7 = bf16[5,66,2048]{2,1,0:T(8,128)(2,1)} collective-permute-done((bf16[5,66,2048]{2,1,0:T(8,128)(2,1)}, bf16[5,66,2048]{2,1,0:T(8,128)(2,1)}, u32[]{:S(2)}, u32[]{:S(2)}) %collective-permute-start.7) | collective-permute-done | bytes 1351712 | tf_op jit(solution)/shard_map/ppermute | solution.py:29
  252.2 3.1 fusion.18
  255.4 1.7 slice.139
  257.1 3.1 fusion.16
  260.2 1.7 slice.140
  261.9 3.1 fusion.14
  264.9 1.7 slice.141
  266.7 3.1 fusion.12
  269.8 12.2 %collective-permute-done.8 = bf16[5,66,2048]{2,1,0:T(8,128)(2,1)S(1)} collective-permute-done((bf16[5,66,2048]{2,1,0:T(8,128)(2,1)}, bf16[5,66,2048]{2,1,0:T(8,128)(2,1)S(1)}, u32[]{:S(2)}, u32[]{:S(2)}) %collective-permute-start.8) | collective-permute-done | bytes 1351712 | tf_op jit(solution)/shard_map/ppermute | solution.py:29
  282.0 7.0 %multiply_convert_fusion = bf16[5,64,2048]{2,1,0:T(8,128)(2,1)S(1)} fusion(f32[5,64,2048]{2,1,0:T(8,128)S(1)} %bitcast.86, bf16[5,66,2048]{2,1,0:T(8,128)(2,1)S(1)} %collective-permute-done.8, bf16[5,66,2048]{2,1,0:T(8,128)(2,1)} %collective-permute-done.7, bf16[5,66,2048]{2,1,0:T(8,128)(2,1)} %collective-permute-done.6, ...), kind=kLoop, calls=%fused_computation.13 | loop fusion | flops 23592960 | bytes 22282268 | tf_op jit(solution)/shard_map/convert_element_type | solution.py:102
  290.2 1.4 slice.142
  291.6 15.8 %fusion.26 = f32[5,2,8,8,1024]{4,3,2,1,0:T(8,128)} fusion(bf16[1024,1024]{1,0:T(8,128)(2,1)S(1)} %copy-done, bf16[5,64,2,1024]{3,1,2,0:T(8,128)(2,1)} %copy-done.14, f32[5,64,2,1024]{3,1,2,0:T(8,128)} %fusion.12, f32[5,64,2,1024]{3,1,2,0:T(8,128)} %fusion.14, f32[5,64,2,1024]{3,1,2,0:T(8,128)} %fusion.16, f32[5,64,2,1024]{3,1,2,0:T(8,128)} %fusion.18, ...), kind=kOutput, calls=%fused_computation.33 | convolution fusion | flops 2694840320 | bytes 23068700 | tf_op jit(solution)/shard_map/...tc,cd->...td/dot_general | solution.py:35
  307.5 1.9 copy.32
  313.0 11.0 %fusion.5 = f32[5,64,2048]{2,1,0:T(8,128)S(1)} fusion(f32[5,64,2048]{2,1,0:T(8,128)S(1)} %bitcast.88, f32[5,64,2048]{2,1,0:T(8,128)S(1)} %slice.159, f32[5,1,2048]{2,1,0:T(1,128)S(1)} %get-tuple-element.7, f32[5,1,2048]{2,1,0:T(1,128)S(1)} %get-tuple-element.6, f32[5,64,2048]{2,1,0:T(8,128)S(1)} %bitcast.87, f32[]{:T(128)} %bitcast.13, f32[]{:T(128)} %bitcast.12, ...), kind=kLoop, calls=%fused_computation.11 | loop fusion | flops 19005440 | bytes 19743004 | tf_op jit(solution)/shard_map/sub | solution.py:106
  (78 shorter events, 17.7 us)
Async XLA Ops:
  0.0 233.1 %copy-start = (bf16[1024,1024]{1,0:T(8,128)(2,1)S(1)}, bf16[1024,1024]{1,0:T(8,128)(2,1)}, u32[]{:S(2)}) copy-start(bf16[1024,1024]{1,0:T(8,128)(2,1)} %param.17) | copy-start | bytes 6291460
  0.0 6.9 %copy-start.18 = (s32[4096]{0:T(1024)S(1)}, s32[4096]{0:T(1024)}, u32[]{:S(2)}) copy-start(s32[4096]{0:T(1024)} %param.20) | copy-start | bytes 49156
  38.1 2.5 copy-start.16
  38.1 2.5 copy-start.17
  40.9 7.2 %collective-permute-start.1 = (bf16[5,1,2048]{2,1,0:T(2,128)(2,1)S(1)}, bf16[5,1,2048]{2,1,0:T(2,128)(2,1)}, u32[]{:S(2)}, u32[]{:S(2)}) collective-permute-start(bf16[5,1,2048]{2,1,0:T(2,128)(2,1)S(1)} %get-tuple-element.11), channel_id=1, source_target_pairs={{1,0},{2,1},{3,2},{4,3},{5,4},{6,5},{7,6},{8,7},{9,8},{10,9},{11,1... | collective-permute-start | bytes 61448 | tf_op jit(solution)/shard_map/ppermute | solution.py:19
  46.4 6.1 %collective-permute-start = (bf16[5,1,2048]{2,1,0:T(2,128)(2,1)S(1)}, bf16[5,1,2048]{2,1,0:T(2,128)(2,1)S(1)}, u32[]{:S(2)}, u32[]{:S(2)}) collective-permute-start(bf16[5,1,2048]{2,1,0:T(2,128)(2,1)S(1)} %get-tuple-element.10), channel_id=1, source_target_pairs={{0,1},{1,2},{2,3},{3,4},{4,5},{5,6},{6,7},{7,8},{8,9},{9,10},{10,1... | collective-permute-start | bytes 61448 | tf_op jit(solution)/shard_map/ppermute | solution.py:17
  46.4 140.9 %copy-start.15 = (bf16[4,64,2048]{2,1,0:T(8,128)(2,1)S(1)}, bf16[4,64,2048]{2,1,0:T(8,128)(2,1)}, u32[]{:S(2)}) copy-start(bf16[4,64,2048]{2,1,0:T(8,128)(2,1)} %get-tuple-element.20) | copy-start | bytes 3145732
  53.0 33.9 %collective-permute-start.2 = (bf16[5,66,2048]{2,1,0:T(8,128)(2,1)S(1)}, bf16[5,66,2048]{2,1,0:T(8,128)(2,1)S(1)}, u32[]{:S(2)}, u32[]{:S(2)}) collective-permute-start(bf16[5,66,2048]{2,1,0:T(8,128)(2,1)S(1)} %pad_maximum_fusion.2), channel_id=1, source_target_pairs={{14,0},{15,1},{0,2},{1,3},{2,4},{3,5},{4,6},{5,7},{6,8},{7,9},{8,1... | collective-permute-start | bytes 4055048 | tf_op jit(solution)/shard_map/ppermute | solution.py:29
  86.8 1.1 copy-start.3
  88.0 32.9 %collective-permute-start.3 = (bf16[5,66,2048]{2,1,0:T(8,128)(2,1)S(1)}, bf16[5,66,2048]{2,1,0:T(8,128)(2,1)S(1)}, u32[]{:S(2)}, u32[]{:S(2)}) collective-permute-start(bf16[5,66,2048]{2,1,0:T(8,128)(2,1)S(1)} %collective-permute-done.2), channel_id=1, source_target_pairs={{14,0},{15,1},{0,2},{1,3},{2,4},{3,5},{4,6},{5,7},{6,8},{7,9},{8,1... | collective-permute-start | bytes 4055048 | tf_op jit(solution)/shard_map/ppermute | solution.py:29
  120.8 1.1 copy-start.6
  122.0 32.0 %collective-permute-start.4 = (bf16[5,66,2048]{2,1,0:T(8,128)(2,1)S(1)}, bf16[5,66,2048]{2,1,0:T(8,128)(2,1)S(1)}, u32[]{:S(2)}, u32[]{:S(2)}) collective-permute-start(bf16[5,66,2048]{2,1,0:T(8,128)(2,1)S(1)} %collective-permute-done.3), channel_id=1, source_target_pairs={{14,0},{15,1},{0,2},{1,3},{2,4},{3,5},{4,6},{5,7},{6,8},{7,9},{8,1... | collective-permute-start | bytes 4055048 | tf_op jit(solution)/shard_map/ppermute | solution.py:29
  153.9 1.2 copy-start.9
  155.1 32.2 %collective-permute-start.5 = (bf16[5,66,2048]{2,1,0:T(8,128)(2,1)S(1)}, bf16[5,66,2048]{2,1,0:T(8,128)(2,1)}, u32[]{:S(2)}, u32[]{:S(2)}) collective-permute-start(bf16[5,66,2048]{2,1,0:T(8,128)(2,1)S(1)} %collective-permute-done.4), channel_id=1, source_target_pairs={{14,0},{15,1},{0,2},{1,3},{2,4},{3,5},{4,6},{5,7},{6,8},{7,9},{8,1... | collective-permute-start | bytes 4055048 | tf_op jit(solution)/shard_map/ppermute | solution.py:29
  187.3 32.5 %collective-permute-start.6 = (bf16[5,66,2048]{2,1,0:T(8,128)(2,1)}, bf16[5,66,2048]{2,1,0:T(8,128)(2,1)}, u32[]{:S(2)}, u32[]{:S(2)}) collective-permute-start(bf16[5,66,2048]{2,1,0:T(8,128)(2,1)} %collective-permute-done.5), channel_id=1, source_target_pairs={{14,0},{15,1},{0,2},{1,3},{2,4},{3,5},{4,6},{5,7},{6,8},{7,9},{8,1... | collective-permute-start | bytes 4055048 | tf_op jit(solution)/shard_map/ppermute | solution.py:29
  219.8 32.4 %collective-permute-start.7 = (bf16[5,66,2048]{2,1,0:T(8,128)(2,1)}, bf16[5,66,2048]{2,1,0:T(8,128)(2,1)}, u32[]{:S(2)}, u32[]{:S(2)}) collective-permute-start(bf16[5,66,2048]{2,1,0:T(8,128)(2,1)} %collective-permute-done.6), channel_id=1, source_target_pairs={{14,0},{15,1},{0,2},{1,3},{2,4},{3,5},{4,6},{5,7},{6,8},{7,9},{8,1... | collective-permute-start | bytes 4055048 | tf_op jit(solution)/shard_map/ppermute | solution.py:29
  223.2 2.2 copy-start.14
  223.7 7.5 %copy-start.19 = (f32[128]{0:T(128)S(1)}, f32[128]{0:T(128)}, u32[]{:S(2)}) copy-start(f32[128]{0:T(128)} %param.21) | copy-start | bytes 1540
  233.1 3.1 copy-start.7
  236.5 3.0 copy-start.10
  252.2 29.8 %collective-permute-start.8 = (bf16[5,66,2048]{2,1,0:T(8,128)(2,1)}, bf16[5,66,2048]{2,1,0:T(8,128)(2,1)S(1)}, u32[]{:S(2)}, u32[]{:S(2)}) collective-permute-start(bf16[5,66,2048]{2,1,0:T(8,128)(2,1)} %collective-permute-done.7), channel_id=1, source_target_pairs={{14,0},{15,1},{0,2},{1,3},{2,4},{3,5},{4,6},{5,7},{6,8},{7,9},{8,1... | collective-permute-start | bytes 4055048 | tf_op jit(solution)/shard_map/ppermute | solution.py:29
  266.7 15.3 %copy-start.1 = (f32[5,2,8,8,1024]{4,3,1,2,0:T(8,128)S(1)}, f32[5,2,8,8,1024]{4,3,1,2,0:T(8,128)}, u32[]{:S(2)}) copy-start(f32[5,2,8,8,1024]{4,3,1,2,0:T(8,128)} %copy.33) | copy-start | bytes 7864324
  266.7 15.3 %copy-start.4 = (bf16[5,66,2048]{2,1,0:T(8,128)(2,1)S(1)}, bf16[5,66,2048]{2,1,0:T(8,128)(2,1)}, u32[]{:S(2)}) copy-start(bf16[5,66,2048]{2,1,0:T(8,128)(2,1)} %copy-done.3) | copy-start | bytes 4055044
  282.0 8.2 %copy-start.12 = (bf16[5,66,2048]{2,1,0:T(8,128)(2,1)}, bf16[5,66,2048]{2,1,0:T(8,128)(2,1)S(1)}, u32[]{:S(2)}) copy-start(bf16[5,66,2048]{2,1,0:T(8,128)(2,1)S(1)} %collective-permute-done.8) | copy-start | bytes 4055044
  289.7 19.7 %collective-permute-start.10 = (bf16[5,1,2048]{2,1,0:T(2,128)(2,1)}, bf16[5,1,2048]{2,1,0:T(2,128)(2,1)S(1)}, u32[]{:S(2)}, u32[]{:S(2)}) collective-permute-start(bf16[5,1,2048]{2,1,0:T(2,128)(2,1)} %get-tuple-element.9), channel_id=1, source_target_pairs={{1,0},{2,1},{3,2},{4,3},{5,4},{6,5},{7,6},{8,7},{9,8},{10,9},{11,1... | collective-permute-start | bytes 61448 | tf_op jit(solution)/shard_map/ppermute | solution.py:19
  289.7 19.7 %collective-permute-start.9 = (bf16[5,1,2048]{2,1,0:T(2,128)(2,1)S(1)}, bf16[5,1,2048]{2,1,0:T(2,128)(2,1)S(1)}, u32[]{:S(2)}, u32[]{:S(2)}) collective-permute-start(bf16[5,1,2048]{2,1,0:T(2,128)(2,1)S(1)} %get-tuple-element.8), channel_id=1, source_target_pairs={{0,1},{1,2},{2,3},{3,4},{4,5},{5,6},{6,7},{7,8},{8,9},{9,10},{10,1... | collective-permute-start | bytes 61448 | tf_op jit(solution)/shard_map/ppermute | solution.py:17
  309.4 1.4 copy-start.11
  309.4 1.8 copy-start.13
  309.9 2.3 copy-start.2
  309.9 2.7 copy-start.5
  309.9 3.1 copy-start.8
where the time goes:
time: 326 us; the launch traced here: 325 us
  waiting for transfers between devices  191 us (59%)
  local copies, waits for them, and re-layouts  58.6 us (18%)
  matrix products  37.8 us (12%)
  other arithmetic  26.7 us (8%)
  starting transfers between devices  6.08 us (2%)
  between operations  4.95 us (2%)
    ppermute x7, waiting for transfers between devices, from_behind(): return lax.ppermute(block, axis, route)  186 us
    dot_general x8, matrix products, tile_apply(): jnp.einsum('...tc,cd->...td', shaped, matrix, preferred_element_type=jnp....  37.8 us
    scatter x1, local copies, waits for them, and re-layouts, on_device(): jnp.zeros((rows * columns,), jnp.bfloat16).at[offsets].set(1, mode='drop')  28.7 us
    sub x1, other arithmetic, on_device(): -divergence - weight_rows[None, :, None] * (wiener_wide * total_src)  11 us
    slice x7, local copies, waits for them, and re-layouts, on_device(): middle = moving[:, 1:-1]  8.88 us
    convert_element_type x1, other arithmetic, on_device(): flux_dec.astype(jnp.bfloat16)  7.01 us
  transfers between devices with their start and end apart: 11, of which 9 were waited for; matrix products, arithmetic and copies ran while one was open for 17% of the time, Pallas kernels for 0%

commit v1 on v0

v1 whole, which is shorter than its diff:
```python
import functools

import jax
import jax.numpy as jnp
from jax import lax
from jax.experimental import pallas as pl
from jax.experimental.pallas import tpu as pltpu
from jax.sharding import PartitionSpec as P

GROUPS = ((0, 1, 2), (3, 4))
PIXEL_CHUNK = 1024
LOW_COLUMNS = 256
VMEM_LIMIT = 40 * 1024 * 1024

F32 = jnp.float32
BF16 = jnp.bfloat16
SMEM = pl.BlockSpec(memory_space=pltpu.SMEM)
VMEM = pl.BlockSpec(memory_space=pltpu.VMEM)
ANY = pl.BlockSpec(memory_space=pl.ANY)
PARAMS = pltpu.CompilerParams(vmem_limit_bytes=VMEM_LIMIT)


def cost(flops, bytes_accessed):
    return pl.CostEstimate(flops=int(flops), bytes_accessed=int(bytes_accessed), transcendentals=0)


def send_order(count):
    return list(range(count - 1, -1, -1))


def keep_kernel(rows, width, a_ref, b_ref, keep_ref, total):
    pixels = a_ref.shape[1]
    tall = total.shape[0]
    total[...] = jnp.zeros_like(total)

    @pl.loop(0, pixels // PIXEL_CHUNK)
    def _(step):
        part = pl.ds(pl.multiple_of(step * PIXEL_CHUNK, PIXEL_CHUNK), PIXEL_CHUNK)
        high = lax.broadcasted_iota(jnp.int32, (tall, PIXEL_CHUNK), 0) == a_ref[:, part]
        low = lax.broadcasted_iota(jnp.int32, (LOW_COLUMNS, PIXEL_CHUNK), 0) == b_ref[:, part]
        total[...] += lax.dot_general(
            high.astype(F32).astype(BF16),
            low.astype(F32).astype(BF16),
            (((1,), (1,)), ((), ())),
            preferred_element_type=F32,
        )

    per_tile = width // LOW_COLUMNS
    for block in range(tall // rows):
        tile, piece = block // per_tile, block % per_tile
        count = total[block * rows : (block + 1) * rows, :]
        keep_ref[tile, :, piece * LOW_COLUMNS : (piece + 1) * LOW_COLUMNS] = jnp.where(
            count > 0, 0.0, 1.0
        ).astype(BF16)


def keep_mask(source_pixels, band_index, rows, columns, width):
    offsets = source_pixels - band_index * rows * columns
    inside = (offsets >= 0) & (offsets < rows * columns)
    row, column = offsets // columns, offsets % columns
    a = jnp.where(inside, (column // LOW_COLUMNS) * rows + row, -1)
    b = column % LOW_COLUMNS
    pixels = source_pixels.shape[0]
    extra = -pixels % PIXEL_CHUNK
    a = jnp.pad(a, (0, extra), constant_values=-1)[None]
    b = jnp.pad(b, (0, extra))[None]
    tall = columns // LOW_COLUMNS * rows
    return pl.pallas_call(
        functools.partial(keep_kernel, rows, width),
        out_shape=jax.ShapeDtypeStruct((columns // width, rows, width), BF16),
        in_specs=[VMEM, VMEM],
        out_specs=VMEM,
        scratch_shapes=[pltpu.VMEM((tall, LOW_COLUMNS), F32)],
        compiler_params=PARAMS,
        cost_estimate=cost(2 * tall * LOW_COLUMNS * (pixels + extra), 4 * rows * columns),
        name="keep",
    )(a, b)


def wiener_kernel(index_ref, first_ref, sky_ref, sim_ref, matrix_ref, out_ref, head_ref, tail_ref, edge_ref):
    field = pl.program_id(0)
    tiles, rows, width = out_ref.shape[1:]

    def apply(source):
        for tile in range(tiles):
            values = source(pl.ds(tile * width, width))
            result = jnp.dot(values, matrix_ref[...], preferred_element_type=F32).astype(BF16)
            out_ref[0, tile] = result
            head = result[:1].astype(F32)
            tail = result[rows - 1 :].astype(F32)
            head_ref[0, tile] = head.astype(BF16)
            tail_ref[0, tile] = tail.astype(BF16)
            edge_ref[0, tile] = jnp.where(first_ref[0] > 0, tail, head).astype(BF16)

    @pl.when(field == 0)
    def _():
        apply(lambda part: sky_ref[:, part])

    @pl.when(field > 0)
    def _():
        apply(lambda part: sim_ref[0, :, part])


def wiener_fields(sim_index, first, sky_maps, sim_sky, matrix):
    rows, columns = sky_maps.shape
    width = matrix.shape[0]
    tiles = columns // width
    fields = sim_index.shape[0] + 1
    own = jnp.concatenate([sim_index[:1], sim_index])
    edge_shape = jax.ShapeDtypeStruct((fields, tiles, 1, width), BF16)
    edge_spec = pl.BlockSpec((1, tiles, 1, width), lambda f, *_: (f, 0, 0, 0))
    return pl.pallas_call(
        wiener_kernel,
        out_shape=[jax.ShapeDtypeStruct((fields, tiles, rows, width), BF16)] + [edge_shape] * 3,
        grid_spec=pltpu.PrefetchScalarGridSpec(
            num_scalar_prefetch=2,
            grid=(fields,),
            in_specs=[
                pl.BlockSpec((rows, columns), lambda f, *_: (0, 0)),
                pl.BlockSpec((1, rows, columns), lambda f, index, *_: (index[f], 0, 0)),
                pl.BlockSpec((width, width), lambda f, *_: (0, 0)),
            ],
            out_specs=[
                pl.BlockSpec((1, tiles, rows, width), lambda f, *_: (f, 0, 0, 0))
            ] + [edge_spec] * 3,
        ),
        compiler_params=PARAMS,
        cost_estimate=cost(2 * fields * rows * columns * width, 4 * fields * rows * columns),
        name="wiener",
    )(own, first, sky_maps, sim_sky, matrix)


def pack_kernel(group, parts, index_ref, row_ref, column_ref, ivf_ref, sim_ref, *refs):
    outs, sems = refs[:parts], refs[parts]
    depth, width = outs[0].shape[1:]
    copies = []
    for d in send_order(parts):
        part = (
            pl.ds(pl.multiple_of(row_ref[d], depth), depth),
            pl.ds(pl.multiple_of(column_ref[d], width), width),
        )
        for place, field in enumerate(group):
            source = ivf_ref.at[part] if field == 0 else sim_ref.at[(index_ref[field - 1],) + part]
            copy = pltpu.make_async_copy(source, outs[d].at[place], sems.at[d, place])
            copy.start()
            copies.append(copy)
    for copy in copies:
        copy.wait()


def pack(group, sim_index, slot_rows, slot_columns, ivf_maps, sim_ivf, depth, width):
    parts = slot_rows.shape[0]
    shape = jax.ShapeDtypeStruct((len(group), depth, width), BF16)
    return pl.pallas_call(
        functools.partial(pack_kernel, group, parts),
        out_shape=[shape] * parts,
        in_specs=[SMEM, SMEM, SMEM, ANY, ANY],
        out_specs=[ANY] * parts,
        scratch_shapes=[pltpu.SemaphoreType.DMA((parts, len(group)))],
        compiler_params=PARAMS,
        cost_estimate=cost(0, 4 * parts * len(group) * depth * width),
        name="pack",
    )(sim_index, slot_rows, slot_columns, ivf_maps, sim_ivf)


def mix_kernel(parts, weights_ref, *refs):
    chunks, outs = refs[:parts], refs[parts:]
    fields, depth, _ = chunks[0].shape
    for place in range(fields):
        stacked = jnp.concatenate([chunk[place] for chunk in chunks], axis=0)
        mixed = jnp.dot(weights_ref[...], stacked, preferred_element_type=F32).astype(BF16)
        for d in range(parts):
            outs[d][place] = mixed[d * depth : (d + 1) * depth]


def mix(weights, chunks):
    parts = len(chunks)
    shape = chunks[0].shape
    size = shape[0] * shape[1] * shape[2]
    return pl.pallas_call(
        functools.partial(mix_kernel, parts),
        out_shape=[jax.ShapeDtypeStruct(shape, BF16)] * parts,
        in_specs=[VMEM] * (parts + 1),
        out_specs=[VMEM] * parts,
        compiler_params=PARAMS,
        cost_estimate=cost(2 * parts * size * weights.shape[0], 4 * parts * size),
        name="mix",
    )(weights, *chunks)


def assemble_kernel(parts, first_ref, row_ref, tile_ref, keep_ref, *refs):
    chunks = refs[:parts]
    out_ref, head_ref, tail_ref, edge_ref = refs[parts:]
    fields, _, rows, _ = out_ref.shape
    depth = chunks[0].shape[1]
    for d in range(parts):
        part = pl.ds(pl.multiple_of(row_ref[d], depth), depth)
        tile = tile_ref[d]
        keep = keep_ref[tile, part, :]
        for place in range(fields):
            out_ref[place, tile, part, :] = chunks[d][place] * keep
    for place in range(fields):
        for tile in range(out_ref.shape[1]):
            head = out_ref[place, tile, 0:16, :].astype(F32)[:2]
            tail = out_ref[place, tile, rows - 16 : rows, :].astype(F32)[14:]
            head_ref[place, tile] = head.astype(BF16)
            tail_ref[place, tile] = tail.astype(BF16)
            edge_ref[place, tile] = jnp.where(first_ref[0] > 0, tail, head).astype(BF16)


def assemble(first, slot_rows, slot_tiles, keep, chunks):
    parts = len(chunks)
    fields, depth, width = chunks[0].shape
    tiles, rows, _ = keep.shape
    edge_shape = jax.ShapeDtypeStruct((fields, tiles, 2, width), BF16)
    return pl.pallas_call(
        functools.partial(assemble_kernel, parts),
        out_shape=[jax.ShapeDtypeStruct((fields, tiles, rows, width), BF16)] + [edge_shape] * 3,
        in_specs=[SMEM] * 3 + [VMEM] * (parts + 1),
        out_specs=[VMEM] * 4,
        compiler_params=PARAMS,
        cost_estimate=cost(fields * tiles * rows * width, 4 * fields * tiles * rows * width),
        name="assemble",
    )(first, slot_rows, slot_tiles, keep, *chunks)


def slope(values):
    rows = values.shape[0]
    line = lax.broadcasted_iota(jnp.int32, values.shape, 0)
    above = jnp.where(line == rows - 1, 0.0, pltpu.roll(values, rows - 1, 0))
    below = jnp.where(line == 0, 0.0, pltpu.roll(values, 1, 0))
    return (above - below) * 0.5


def home_kernel(group, uses, earlier, final, *refs):
    refs = list(refs)
    sums_ref, wiener_ref, matrix_ref = refs[:3]
    before = refs[3 : 3 + 3 * earlier]
    rest = refs[3 + 3 * earlier :]
    fields, tiles, rows, width = sums_ref.shape
    totals = []
    for tile in range(tiles):
        ra = dec = src = None
        for place, field in enumerate(group):
            share = 1.0 if field == 0 else -1.0 / uses
            sums = sums_ref[place, tile]
            grad = jnp.dot(sums, matrix_ref[...], preferred_element_type=F32)
            wide = sums.astype(F32)
            weight = wiener_ref[field, tile].astype(F32) * share
            terms = weight * grad, weight * slope(wide), weight * wide
            if ra is None:
                ra, dec, src = terms
            else:
                ra, dec, src = ra + terms[0], dec + terms[1], src + terms[2]
        if earlier:
            ra, dec, src = ra + before[0][tile], dec + before[1][tile], src + before[2][tile]
        if not final:
            rest[0][tile], rest[1][tile], rest[2][tile] = ra, dec, src
        else:
            response_ref, out_ref = rest
            high = ra.astype(BF16)
            low = (ra - high.astype(F32)).astype(BF16)
            both = jnp.dot(
                jnp.concatenate([high, low], axis=0), matrix_ref[...], preferred_element_type=F32
            )
            divergence = both[:rows] + both[rows:] + slope(dec)
            out_ref[:, tile * width : (tile + 1) * width] = -divergence - response_ref[...] * src


def home(group, uses, sums, wiener, matrix, before, response, final):
    fields, tiles, rows, width = sums.shape
    shape = jax.ShapeDtypeStruct((tiles, rows, width), F32)
    out_shape = jax.ShapeDtypeStruct((rows, tiles * width), F32) if final else [shape] * 3
    operands = [sums, wiener, matrix, *before] + ([response] if final else [])
    return pl.pallas_call(
        functools.partial(home_kernel, group, uses, bool(before), final),
        out_shape=out_shape,
        in_specs=[VMEM] * len(operands),
        out_specs=VMEM if final else [VMEM] * 3,
        compiler_params=PARAMS,
        cost_estimate=cost(
            2 * (fields + 2 * final) * tiles * rows * width * width, 16 * tiles * rows * width
        ),
        name="home",
    )(*operands)


def rim_kernel(groups, uses, flags_ref, out_in_ref, w_head, w_tail, w_lo, w_hi, *refs):
    out_ref = refs[-1]
    tiles, width = w_head.shape[1], w_head.shape[3]
    side = pl.program_id(0)
    out_ref[...] = out_in_ref[...]

    def terms(own_w, far_w, pick):
        for tile in range(tiles):
            inner = outer = 0.0
            for number, group in enumerate(groups):
                s_head, s_tail, s_lo, s_hi = refs[4 * number : 4 * number + 4]
                for place, field in enumerate(group):
                    share = (1.0 if field == 0 else -1.0 / uses) * 0.25
                    near, beyond, own = pick(s_head, s_tail, s_lo, s_hi, place, tile)
                    inner += own_w[field, tile].astype(F32) * near * share
                    outer += far_w[field, tile].astype(F32) * (own - beyond) * share
            yield pl.ds(tile * width, width), inner, outer

    @pl.when((side == 0) & (flags_ref[0] > 0))
    def _():
        def pick(s_head, s_tail, s_lo, s_hi, place, tile):
            far = s_lo[place, tile].astype(F32)
            return far[1:2], far[0:1], s_head[place, tile].astype(F32)[0:1]

        for part, inner, outer in terms(w_head, w_lo, pick):
            out_ref[1:2, part] = out_ref[1:2, part] - inner
            out_ref[0:1, part] = out_ref[0:1, part] + outer

    @pl.when((side == 1) & (flags_ref[1] > 0))
    def _():
        def pick(s_head, s_tail, s_lo, s_hi, place, tile):
            far = s_hi[place, tile].astype(F32)
            return far[0:1], far[1:2], s_tail[place, tile].astype(F32)[1:2]

        last = out_ref.shape[0] - 1
        for part, inner, outer in terms(w_tail, w_hi, pick):
            out_ref[last - 1 : last, part] = out_ref[last - 1 : last, part] - inner
            out_ref[last : last + 1, part] = out_ref[last : last + 1, part] + outer


def rim(groups, uses, flags, out, wiener_rims, sum_rims):
    rows, columns = out.shape
    block = pl.BlockSpec((8, columns), lambda side: (side * (rows // 8 - 1), 0))
    small = [*wiener_rims] + [array for rims in sum_rims for array in rims]

    def whole(array):
        zeros = (0,) * array.ndim
        return pl.BlockSpec(array.shape, lambda side: zeros)

    return pl.pallas_call(
        functools.partial(rim_kernel, groups, uses),
        out_shape=jax.ShapeDtypeStruct(out.shape, out.dtype),
        grid=(2,),
        in_specs=[SMEM, block] + [whole(array) for array in small],
        out_specs=block,
        input_output_aliases={1: 0},
        compiler_params=PARAMS,
        cost_estimate=cost(0, 64 * columns),
        name="rim",
    )(flags, out, *small)


def on_device(
    sky_maps,
    ivf_maps,
    sim_sky,
    sim_ivf,
    ra_wiener,
    ra_gradient,
    pair_table,
    sim_index,
    source_pixels,
    response,
):
    splits = pair_table.shape[0]
    uses = sim_index.shape[0]
    axis_count = lax.axis_size("sim")
    bands = axis_count // splits
    device = lax.axis_index("sim")
    logical = (device - bands // 2) % axis_count
    band = logical % bands
    rows, columns = sky_maps.shape
    width = ra_gradient.shape[0]
    tiles = columns // width
    depth = rows * tiles // splits

    place, lane = device // bands, device % bands
    slots = place ^ jnp.arange(splits)
    slot_rows = (slots // tiles * depth).astype(jnp.int32)
    slot_tiles = (slots % tiles).astype(jnp.int32)
    slot_columns = slot_tiles * width

    def swap(block, d):
        if d == 0:
            return block
        pairs = [
            (g * bands + u, (g ^ d) * bands + u) for g in range(splits) for u in range(bands)
        ]
        return lax.ppermute(block, "sim", pairs)

    def exchange(blocks):
        moved = {d: swap(blocks[d], d) for d in send_order(splits)}
        return [moved[d] for d in range(splits)]

    def neighbours(head, tail, edge):
        if bands == 2:
            pairs = [((k + 1) % axis_count, k) if (k - 1) % 2 == 0 else ((k - 1) % axis_count, k)
                     for k in range(axis_count)]
            got = lax.ppermute(edge, "sim", pairs)
            return got, got
        ahead = [(k, (k + 1) % axis_count) for k in range(axis_count)]
        back = [((k + 1) % axis_count, k) for k in range(axis_count)]
        return lax.ppermute(tail, "sim", ahead), lax.ppermute(head, "sim", back)

    first = (band == 0).astype(jnp.int32)[None]
    flags = jnp.stack([band > 0, band < bands - 1]).astype(jnp.int32)

    split_of = (slots - (lane < bands // 2)) % splits
    pairs = jnp.where(split_of[:, None] == split_of[None], 0, pair_table[split_of][:, split_of])
    weights = jnp.kron(pairs.astype(F32), jnp.eye(depth, dtype=F32)).astype(BF16)

    sent = [
        pack(group, sim_index, slot_rows, slot_columns, ivf_maps, sim_ivf, depth, width)
        for group in GROUPS
    ]
    arrived = [exchange(blocks) for blocks in sent]
    keep = keep_mask(source_pixels, band, rows, columns, width)
    wiener, *w_edges = wiener_fields(sim_index, first, sky_maps, sim_sky, ra_wiener)
    w_lo, w_hi = neighbours(*w_edges)
    returned = [exchange(mix(weights, blocks)) for blocks in arrived]
    band_response = lax.dynamic_slice_in_dim(response, band * rows, rows)[:, None]
    before, sum_rims = [], []
    for number, group in enumerate(GROUPS):
        sums, *edges = assemble(first, slot_rows, slot_tiles, keep, returned[number])
        s_lo, s_hi = neighbours(*edges)
        sum_rims.append([edges[0], edges[1], s_lo, s_hi])
        final = number == len(GROUPS) - 1
        before = home(group, uses, sums, wiener, ra_gradient, before, band_response, final)
    return rim(GROUPS, uses, flags, before, [w_edges[0], w_edges[1], w_lo, w_hi], sum_rims)


def solution(mesh):
    in_specs = (
        P(("patch", "sim"), None),
        P(("patch", "sim"), None),
        P(None, ("patch", "sim"), None),
        P(None, ("patch", "sim"), None),
        P(),
        P(),
        P(),
        P(),
        P("patch"),
        P("patch"),
    )
    out_specs = P(("patch", "sim"), None)
    return jax.shard_map(
        on_device, mesh=mesh, in_specs=in_specs, out_specs=out_specs, check_vma=False
    )
```

time: 326 us -> 90.8 us (0.28)
  waiting for transfers between devices: 191 us -> 6.6 us
  local copies, waits for them, and re-layouts: 58.6 us -> 9.95 us
  starting transfers between devices: 6.08 us -> 52 us
  matrix products: 37.8 us -> 0 us
  other arithmetic: 26.7 us -> 0.47 us
  Pallas kernels: 0 us -> 19.8 us
  between operations: 4.95 us -> 0.33 us
    ppermute x11 -> x31, waiting for transfers between devices: 191 us -> 6.6 us  [the longest x28 6.42 us: swap(): return lax.ppermute(block, 'sim', pairs)]
    ppermute x11 -> x31, starting transfers between devices: 6.08 us -> 52 us  [the longest x28 47.3 us: swap(): return lax.ppermute(block, 'sim', pairs)]
    dot_general x8 -> x0, matrix products: 37.8 us -> none  [tile_apply(): jnp.einsum('...tc,cd->...td', shaped, matrix, preferred_element_type=jnp....]
    scatter x1 -> x0, local copies, waits for them, and re-layouts: 28.7 us -> none  [on_device(): jnp.zeros((rows * columns,), jnp.bfloat16).at[offsets].set(1, mode='drop')]
    pallas_call x0 -> x11, Pallas kernels: none -> 19.8 us  [the longest x2 5.68 us: home(): pl.pallas_call(functools.partial(home_kernel, group, uses, bool(before),...]
    sub x3 -> x0, other arithmetic: 12.5 us -> none  [the longest x1 11 us: on_device(): -divergence - weight_rows[None, :, None] * (wiener_wide * total_src)]
    slice x10 -> x0, local copies, waits for them, and re-layouts: 9.9 us -> none  [the longest x7 8.88 us: on_device(): middle = moving[:, 1:-1]]
    convert_element_type x3 -> x4, other arithmetic: 8.16 us -> 0.27 us  [the longest x1 0.11 us: on_device(): jnp.kron(pairs.astype(F32), jnp.eye(depth, dtype=F32)).astype(BF16)]
  transfers between devices with their start and end apart: 11 -> 31, of which waited for: 9 -> 4; matrix products, arithmetic and copies ran while one was open for 17% -> 2% of each run, Pallas kernels for 0% -> 19%
where the time goes in v1:
time: 90.8 us; the launch traced here: 89.1 us
  starting transfers between devices  52 us (57%)
  Pallas kernels  19.8 us (22%)
  local copies, waits for them, and re-layouts  9.95 us (11%)
  waiting for transfers between devices  6.6 us (7%)
    ppermute x28, starting transfers between devices, swap(): return lax.ppermute(block, 'sim', pairs)  47.3 us
    unnamed x48, local copies, waits for them, and re-layouts  8.34 us
    ppermute x28, waiting for transfers between devices, swap(): return lax.ppermute(block, 'sim', pairs)  6.42 us
    pallas_call x2, Pallas kernels, home(): pl.pallas_call(functools.partial(home_kernel, group, uses, bool(before),...  5.68 us
    pallas_call x1, Pallas kernels, wiener_fields(): pl.pallas_call(wiener_kernel, out_shape=[jax.ShapeDtypeStruct((fields, ti...  4.91 us
    ppermute x3, starting transfers between devices, neighbours(): got = lax.ppermute(edge, 'sim', pairs)  4.64 us
    pallas_call x2, Pallas kernels, pack(): pl.pallas_call(functools.partial(pack_kernel, group, parts), out_shape=[s...  2.97 us
    pallas_call x1, Pallas kernels, keep_mask(): pl.pallas_call(functools.partial(keep_kernel, rows, width), out_shape=jax...  2.02 us
  transfers between devices with their start and end apart: 31, of which 4 were waited for; matrix products, arithmetic and copies ran while one was open for 2% of the time, Pallas kernels for 19%

profile of v1, /device:TPU:0, one launch (start us, length us, event | category | flops | bytes accessed | tf_op | source)
XLA Modules:
  0.0 89.1 jit_solution(12553517788243489328)
XLA Ops:
  0.0 1.6 %copy-done.2 = bf16[8,64,2048]{2,1,0:T(8,128)(2,1)S(1)} copy-done((bf16[8,64,2048]{2,1,0:T(8,128)(2,1)S(1)}, bf16[8,64,2048]{2,1,0:T(8,128)(2,1)}, u32[]{:S(2)}) %copy-start.2) | copy-done | bytes 2097176
  3.2 1.5 %pack.2 = (bf16[2,16,1024]{2,1,0:T(8,128)(2,1)S(1)}, bf16[2,16,1024]{2,1,0:T(8,128)(2,1)}, bf16[2,16,1024]{2,1,0:T(8,128)(2,1)}, bf16[2,16,1024]{2,1,0:T(8,128)(...) custom-call(s32[4]{0:T(128)S(1)} %copy-done.6, ...), custom_call_target="tpu_custom_call" | custom-call | bytes 1048576 | tf_op jit(solution)/shard_map/pack/pallas_call | solution.py:154
  4.8 3.0 %collective-permute-start = (bf16[2,16,1024]{2,1,0:T(8,128)(2,1)}, bf16[2,16,1024]{2,1,0:T(8,128)(2,1)S(1)}, u32[]{:S(2)}, u32[]{:S(2)}) collective-permute-start(bf16[2,16,1024]{2,1,0:T(8,128)(2,1)} %get-tuple-element.53), channel_id=1, source_target_pairs={{0,2},{1,3},{2,0},{3,1},{4,6},{5,7},{6,4},{7,5},{8,10},{9,11},{10,... | collective-permute-start | bytes 196616 | tf_op jit(solution)/shard_map/ppermute | solution.py:386
  7.9 1.6 %collective-permute-start.1 = (bf16[2,16,1024]{2,1,0:T(8,128)(2,1)}, bf16[2,16,1024]{2,1,0:T(8,128)(2,1)S(1)}, u32[]{:S(2)}, u32[]{:S(2)}) collective-permute-start(bf16[2,16,1024]{2,1,0:T(8,128)(2,1)} %get-tuple-element.54), channel_id=1, source_target_pairs={{0,4},{1,5},{2,6},{3,7},{4,0},{5,1},{6,2},{7,3},{8,12},{9,13},{10,... | collective-permute-start | bytes 196616 | tf_op jit(solution)/shard_map/ppermute | solution.py:386
  9.5 3.0 %collective-permute-start.3 = (bf16[2,16,1024]{2,1,0:T(8,128)(2,1)}, bf16[2,16,1024]{2,1,0:T(8,128)(2,1)S(1)}, u32[]{:S(2)}, u32[]{:S(2)}) collective-permute-start(bf16[2,16,1024]{2,1,0:T(8,128)(2,1)} %get-tuple-element.56), channel_id=1, source_target_pairs={{0,8},{1,9},{2,10},{3,11},{4,12},{5,13},{6,14},{7,15},{8,0},{9,1},... | collective-permute-start | bytes 196616 | tf_op jit(solution)/shard_map/ppermute | solution.py:386
  12.4 1.3 %collective-permute-start.4 = (bf16[2,16,1024]{2,1,0:T(8,128)(2,1)}, bf16[2,16,1024]{2,1,0:T(8,128)(2,1)S(1)}, u32[]{:S(2)}, u32[]{:S(2)}) collective-permute-start(bf16[2,16,1024]{2,1,0:T(8,128)(2,1)} %get-tuple-element.57), channel_id=1, source_target_pairs={{0,10},{1,11},{2,8},{3,9},{4,14},{5,15},{6,12},{7,13},{8,2},{9,3},... | collective-permute-start | bytes 196616 | tf_op jit(solution)/shard_map/ppermute | solution.py:386
  13.8 1.4 %pack.3 = (bf16[3,16,1024]{2,1,0:T(8,128)(2,1)S(1)}, bf16[3,16,1024]{2,1,0:T(8,128)(2,1)S(1)}, bf16[3,16,1024]{2,1,0:T(8,128)(2,1)S(1)}, bf16[3,16,1024]{2,1,0:T...) custom-call(s32[4]{0:T(128)S(1)} %copy-done.7, ...), custom_call_target="tpu_custom_call" | custom-call | bytes 1572864 | tf_op jit(solution)/shard_map/pack/pallas_call | solution.py:154
  19.0 3.6 %collective-permute-start.5 = (bf16[2,16,1024]{2,1,0:T(8,128)(2,1)}, bf16[2,16,1024]{2,1,0:T(8,128)(2,1)S(1)}, u32[]{:S(2)}, u32[]{:S(2)}) collective-permute-start(bf16[2,16,1024]{2,1,0:T(8,128)(2,1)} %copy-done.19), channel_id=1, source_target_pairs={{0,12},{1,13},{2,14},{3,15},{4,8},{5,9},{6,10},{7,11},{8,4},{9,5},... | collective-permute-start | bytes 196616 | tf_op jit(solution)/shard_map/ppermute | solution.py:386
  22.6 1.7 %collective-permute-start.14 = (bf16[3,16,1024]{2,1,0:T(8,128)(2,1)}, bf16[3,16,1024]{2,1,0:T(8,128)(2,1)S(1)}, u32[]{:S(2)}, u32[]{:S(2)}) collective-permute-start(bf16[3,16,1024]{2,1,0:T(8,128)(2,1)} %copy-done.17), channel_id=1, source_target_pairs={{0,2},{1,3},{2,0},{3,1},{4,6},{5,7},{6,4},{7,5},{8,10},{9,11},{10,... | collective-permute-start | bytes 294920 | tf_op jit(solution)/shard_map/ppermute | solution.py:386
  24.3 1.6 %copy-done.8 = bf16[8,64,2048]{2,1,0:T(8,128)(2,1)S(1)} copy-done((bf16[8,64,2048]{2,1,0:T(8,128)(2,1)S(1)}, bf16[8,64,2048]{2,1,0:T(8,128)(2,1)}, u32[]{:S(2)}) %copy-start.8) | copy-done | bytes 2097176
  25.9 1.6 %copy-done.9 = bf16[1024,1024]{1,0:T(8,128)(2,1)S(1)} copy-done((bf16[1024,1024]{1,0:T(8,128)(2,1)S(1)}, bf16[1024,1024]{1,0:T(8,128)(2,1)}, u32[]{:S(2)}) %copy-start.9) | copy-done | bytes 2097176
  27.5 4.9 %wiener.1 = (bf16[5,2,64,1024]{3,2,1,0:T(8,128)(2,1)S(1)}, bf16[5,2,1,1024]{3,2,1,0:T(2,128)(2,1)S(1)}, bf16[5,2,1,1024]{3,2,1,0:T(2,128)(2,1)S(1)}, bf16[5,2,1,1024]{3,2,1,0:T(2,128)(2,1)S(1)}) custom-call(s32[5]{0:T(128)S(1)} %pad_add_fusion.index_ref, s32[1]{0:T(128)} %bitcast.2.first_ref, bf16[64,2048]{1,0:T(8,128)(2,1)S(1)} %copy-done.10, ...), custom_call_target="tpu_custom_call" | custom-call | flops 1342177280 | bytes 2621440 | tf_op jit(solution)/shard_map/wiener/pallas_call | solution.py:112
  32.5 1.8 %collective-permute-start.16 = (bf16[3,16,1024]{2,1,0:T(8,128)(2,1)S(1)}, bf16[3,16,1024]{2,1,0:T(8,128)(2,1)S(1)}, u32[]{:S(2)}, u32[]{:S(2)}) collective-permute-start(bf16[3,16,1024]{2,1,0:T(8,128)(2,1)S(1)} %copy-done.14), channel_id=1, source_target_pairs={{0,6},{1,7},{2,4},{3,5},{4,2},{5,3},{6,0},{7,1},{8,14},{9,15},{10,... | collective-permute-start | bytes 294920 | tf_op jit(solution)/shard_map/ppermute | solution.py:386
  34.4 2.4 %collective-permute-start.17 = (bf16[3,16,1024]{2,1,0:T(8,128)(2,1)S(1)}, bf16[3,16,1024]{2,1,0:T(8,128)(2,1)S(1)}, u32[]{:S(2)}, u32[]{:S(2)}) collective-permute-start(bf16[3,16,1024]{2,1,0:T(8,128)(2,1)S(1)} %copy-done.12), channel_id=1, source_target_pairs={{0,8},{1,9},{2,10},{3,11},{4,12},{5,13},{6,14},{7,15},{8,0},{9,1},... | collective-permute-start | bytes 294920 | tf_op jit(solution)/shard_map/ppermute | solution.py:386
  36.8 1.6 %collective-permute-start.18 = (bf16[3,16,1024]{2,1,0:T(8,128)(2,1)S(1)}, bf16[3,16,1024]{2,1,0:T(8,128)(2,1)S(1)}, u32[]{:S(2)}, u32[]{:S(2)}) collective-permute-start(bf16[3,16,1024]{2,1,0:T(8,128)(2,1)S(1)} %get-tuple-element.75), channel_id=1, source_target_pairs={{0,10},{1,11},{2,8},{3,9},{4,14},{5,15},{6,12},{7,13},{8,2},{9,3},... | collective-permute-start | bytes 294920 | tf_op jit(solution)/shard_map/ppermute | solution.py:386
  38.4 3.6 %collective-permute-start.19 = (bf16[3,16,1024]{2,1,0:T(8,128)(2,1)S(1)}, bf16[3,16,1024]{2,1,0:T(8,128)(2,1)S(1)}, u32[]{:S(2)}, u32[]{:S(2)}) collective-permute-start(bf16[3,16,1024]{2,1,0:T(8,128)(2,1)S(1)} %get-tuple-element.76), channel_id=1, source_target_pairs={{0,12},{1,13},{2,14},{3,15},{4,8},{5,9},{6,10},{7,11},{8,4},{9,5},... | collective-permute-start | bytes 294920 | tf_op jit(solution)/shard_map/ppermute | solution.py:386
  43.0 1.6 %collective-permute-start.7 = (bf16[2,16,1024]{2,1,0:T(8,128)(2,1)}, bf16[2,16,1024]{2,1,0:T(8,128)(2,1)S(1)}, u32[]{:S(2)}, u32[]{:S(2)}) collective-permute-start(bf16[2,16,1024]{2,1,0:T(8,128)(2,1)} %get-tuple-element.61), channel_id=1, source_target_pairs={{0,2},{1,3},{2,0},{3,1},{4,6},{5,7},{6,4},{7,5},{8,10},{9,11},{10,... | collective-permute-start | bytes 196616 | tf_op jit(solution)/shard_map/ppermute | solution.py:386
  44.6 2.1 %collective-permute-done.17.refs_4_ = bf16[3,16,1024]{2,1,0:T(8,128)(2,1)S(1)} collective-permute-done((bf16[3,16,1024]{2,1,0:T(8,128)(2,1)S(1)}, bf16[3,16,1024]{2,1,0:T(8,128)(2,1)S(1)}, u32[]{:S(2)}, u32[]{:S(2)}) %collective-permute-start.17) | collective-permute-done | bytes 98336 | tf_op jit(solution)/shard_map/ppermute | solution.py:386
  46.7 1.1 %collective-permute-start.8 = (bf16[2,16,1024]{2,1,0:T(8,128)(2,1)}, bf16[2,16,1024]{2,1,0:T(8,128)(2,1)S(1)}, u32[]{:S(2)}, u32[]{:S(2)}) collective-permute-start(bf16[2,16,1024]{2,1,0:T(8,128)(2,1)} %get-tuple-element.62), channel_id=1, source_target_pairs={{0,4},{1,5},{2,6},{3,7},{4,0},{5,1},{6,2},{7,3},{8,12},{9,13},{10,... | collective-permute-start | bytes 196616 | tf_op jit(solution)/shard_map/ppermute | solution.py:386
  47.8 4.0 %collective-permute-done.18.refs_5_ = bf16[3,16,1024]{2,1,0:T(8,128)(2,1)S(1)} collective-permute-done((bf16[3,16,1024]{2,1,0:T(8,128)(2,1)S(1)}, bf16[3,16,1024]{2,1,0:T(8,128)(2,1)S(1)}, u32[]{:S(2)}, u32[]{:S(2)}) %collective-permute-start.18) | collective-permute-done | bytes 98336 | tf_op jit(solution)/shard_map/ppermute | solution.py:386
  51.8 2.4 %collective-permute-start.10 = (bf16[2,16,1024]{2,1,0:T(8,128)(2,1)}, bf16[2,16,1024]{2,1,0:T(8,128)(2,1)S(1)}, u32[]{:S(2)}, u32[]{:S(2)}) collective-permute-start(bf16[2,16,1024]{2,1,0:T(8,128)(2,1)} %get-tuple-element.64), channel_id=1, source_target_pairs={{0,8},{1,9},{2,10},{3,11},{4,12},{5,13},{6,14},{7,15},{8,0},{9,1},... | collective-permute-start | bytes 196616 | tf_op jit(solution)/shard_map/ppermute | solution.py:386
  54.4 2.8 %collective-permute-start.11 = (bf16[2,16,1024]{2,1,0:T(8,128)(2,1)S(1)}, bf16[2,16,1024]{2,1,0:T(8,128)(2,1)S(1)}, u32[]{:S(2)}, u32[]{:S(2)}) collective-permute-start(bf16[2,16,1024]{2,1,0:T(8,128)(2,1)S(1)} %get-tuple-element.65), channel_id=1, source_target_pairs={{0,10},{1,11},{2,8},{3,9},{4,14},{5,15},{6,12},{7,13},{8,2},{9,3},... | collective-permute-start | bytes 196616 | tf_op jit(solution)/shard_map/ppermute | solution.py:386
  57.5 1.2 %collective-permute-start.12 = (bf16[2,16,1024]{2,1,0:T(8,128)(2,1)S(1)}, bf16[2,16,1024]{2,1,0:T(8,128)(2,1)S(1)}, u32[]{:S(2)}, u32[]{:S(2)}) collective-permute-start(bf16[2,16,1024]{2,1,0:T(8,128)(2,1)S(1)} %get-tuple-element.66), channel_id=1, source_target_pairs={{0,12},{1,13},{2,14},{3,15},{4,8},{5,9},{6,10},{7,11},{8,4},{9,5},... | collective-permute-start | bytes 196616 | tf_op jit(solution)/shard_map/ppermute | solution.py:386
  58.7 3.6 %collective-permute-start.13 = (bf16[2,16,1024]{2,1,0:T(8,128)(2,1)S(1)}, bf16[2,16,1024]{2,1,0:T(8,128)(2,1)S(1)}, u32[]{:S(2)}, u32[]{:S(2)}) collective-permute-start(bf16[2,16,1024]{2,1,0:T(8,128)(2,1)S(1)} %get-tuple-element.67), channel_id=1, source_target_pairs={{0,14},{1,15},{2,12},{3,13},{4,10},{5,11},{6,8},{7,9},{8,6},{9,7},... | collective-permute-start | bytes 196616 | tf_op jit(solution)/shard_map/ppermute | solution.py:386
  63.0 3.0 %collective-permute-start.23 = (bf16[3,16,1024]{2,1,0:T(8,128)(2,1)S(1)}, bf16[3,16,1024]{2,1,0:T(8,128)(2,1)S(1)}, u32[]{:S(2)}, u32[]{:S(2)}) collective-permute-start(bf16[3,16,1024]{2,1,0:T(8,128)(2,1)S(1)} %get-tuple-element.81), channel_id=1, source_target_pairs={{0,6},{1,7},{2,4},{3,5},{4,2},{5,3},{6,0},{7,1},{8,14},{9,15},{10,... | collective-permute-start | bytes 294920 | tf_op jit(solution)/shard_map/ppermute | solution.py:386
  66.8 4.7 %collective-permute-start.25 = (bf16[3,16,1024]{2,1,0:T(8,128)(2,1)S(1)}, bf16[3,16,1024]{2,1,0:T(8,128)(2,1)S(1)}, u32[]{:S(2)}, u32[]{:S(2)}) collective-permute-start(bf16[3,16,1024]{2,1,0:T(8,128)(2,1)S(1)} %get-tuple-element.83), channel_id=1, source_target_pairs={{0,10},{1,11},{2,8},{3,9},{4,14},{5,15},{6,12},{7,13},{8,2},{9,3},... | collective-permute-start | bytes 294920 | tf_op jit(solution)/shard_map/ppermute | solution.py:386
  71.5 2.2 %collective-permute-start.27 = (bf16[3,16,1024]{2,1,0:T(8,128)(2,1)S(1)}, bf16[3,16,1024]{2,1,0:T(8,128)(2,1)S(1)}, u32[]{:S(2)}, u32[]{:S(2)}) collective-permute-start(bf16[3,16,1024]{2,1,0:T(8,128)(2,1)S(1)} %get-tuple-element.85), channel_id=1, source_target_pairs={{0,14},{1,15},{2,12},{3,13},{4,10},{5,11},{6,8},{7,9},{8,6},{9,7},... | collective-permute-start | bytes 294920 | tf_op jit(solution)/shard_map/ppermute | solution.py:386
  73.6 2.0 %keep.1.keep_ref = bf16[2,64,1024]{2,1,0:T(8,128)(2,1)S(1)} custom-call(s32[1,4096]{1,0:T(1,128)S(1)} %bitcast.17, s32[1,4096]{1,0:T(1,128)S(1)} %bitcast.16), custom_call_target="tpu_custom_call" | custom-call | flops 1073741824 | bytes 524288 | tf_op jit(solution)/shard_map/keep/pallas_call | solution.py:68
  76.4 4.4 %collective-permute-start.30 = (bf16[2,2,2,1024]{3,2,1,0:T(2,128)(2,1)S(1)}, bf16[2,2,2,1024]{3,2,1,0:T(2,128)(2,1)S(1)}, u32[]{:S(2)}, u32[]{:S(2)}) collective-permute-start(bf16[2,2,2,1024]{3,2,1,0:T(2,128)(2,1)S(1)} %get-tuple-element.98), channel_id=1, source_target_pairs={{15,0},{2,1},{1,2},{4,3},{3,4},{6,5},{5,6},{8,7},{7,8},{10,9},{9,1... | collective-permute-start | bytes 49160 | tf_op jit(solution)/shard_map/ppermute | solution.py:396
  81.6 2.5 %home.2 = (f32[2,64,1024]{2,1,0:T(8,128)S(1)}, f32[2,64,1024]{2,1,0:T(8,128)S(1)}, f32[2,64,1024]{2,1,0:T(8,128)S(1)}) custom-call(bf16[3,2,64,1024]{3,2,1,0:T(8,128)(2,1)S(1)} %get-tuple-element.86.refs_0_, bf16[5,2,64,1024]{3,2,1,0:T(8,128)(2,1)S(1)} %get-tuple-element.69.refs_1_, bf16[1024,1024]{1,0:T(8,128)(2,1)S(1)} %copy-done.1), custom_call_target="tpu_custom_call" | custom-call | flops 805306368 | bytes 2097152 | tf_op jit(solution)/shard_map/home/pallas_call | solution.py:275
  84.1 3.2 %home.3.out_in_ref = f32[64,2048]{1,0:T(8,128)} custom-call(bf16[2,2,64,1024]{3,2,1,0:T(8,128)(2,1)S(1)} %get-tuple-element.68.refs_0_, bf16[5,2,64,1024]{3,2,1,0:T(8,128)(2,1)S(1)} %get-tuple-element.69.refs_1_, bf16[1024,1024]{1,0:T(8,128)(2,1)S(1)} %copy-done.1, f32[2,64,1024]{2,1,0:T(8,128)S(1)} %get-tuple-element.87.refs_3_, ...), custom_call_target="tpu_custom_call" | custom-call | flops 1073741824 | bytes 2097152 | tf_op jit(solution)/shard_map/home/pallas_call | solution.py:275
  87.5 1.6 %rim.1 = f32[64,2048]{1,0:T(8,128)} custom-call(s32[2]{0:T(128)S(1)} %add_convert_fusion.flags_ref, f32[64,2048]{1,0:T(8,128)} %home.3.out_in_ref, bf16[5,2,1,1024]{3,2,1,0:T(2,128)(2,1)S(1)} %get-tuple-element.90.w_head, bf16[5,2,1,1024]{3,2,1,0:T(2,128)(2,1)S(1)} %get-tuple-element.91.w_tail, ...), custom_call_target="tpu_custom_call", output_to_operand_aliasing={{}: (1, {})} | custom-call | bytes 131072 | tf_op jit(solution)/shard_map/rim/pallas_call | solution.py:337
  (107 shorter events, 10.3 us)
Async XLA Ops:
  4.8 14.1 %collective-permute-start = (bf16[2,16,1024]{2,1,0:T(8,128)(2,1)}, bf16[2,16,1024]{2,1,0:T(8,128)(2,1)S(1)}, u32[]{:S(2)}, u32[]{:S(2)}) collective-permute-start(bf16[2,16,1024]{2,1,0:T(8,128)(2,1)} %get-tuple-element.53), channel_id=1, source_target_pairs={{0,2},{1,3},{2,0},{3,1},{4,6},{5,7},{6,4},{7,5},{8,10},{9,11},{10,... | collective-permute-start | bytes 196616 | tf_op jit(solution)/shard_map/ppermute | solution.py:386
  7.9 14.7 %collective-permute-start.1 = (bf16[2,16,1024]{2,1,0:T(8,128)(2,1)}, bf16[2,16,1024]{2,1,0:T(8,128)(2,1)S(1)}, u32[]{:S(2)}, u32[]{:S(2)}) collective-permute-start(bf16[2,16,1024]{2,1,0:T(8,128)(2,1)} %get-tuple-element.54), channel_id=1, source_target_pairs={{0,4},{1,5},{2,6},{3,7},{4,0},{5,1},{6,2},{7,3},{8,12},{9,13},{10,... | collective-permute-start | bytes 196616 | tf_op jit(solution)/shard_map/ppermute | solution.py:386
  9.5 13.2 %collective-permute-start.2 = (bf16[2,16,1024]{2,1,0:T(8,128)(2,1)}, bf16[2,16,1024]{2,1,0:T(8,128)(2,1)S(1)}, u32[]{:S(2)}, u32[]{:S(2)}) collective-permute-start(bf16[2,16,1024]{2,1,0:T(8,128)(2,1)} %get-tuple-element.55), channel_id=1, source_target_pairs={{0,6},{1,7},{2,4},{3,5},{4,2},{5,3},{6,0},{7,1},{8,14},{9,15},{10,... | collective-permute-start | bytes 196616 | tf_op jit(solution)/shard_map/ppermute | solution.py:386
  9.5 22.9 %collective-permute-start.3 = (bf16[2,16,1024]{2,1,0:T(8,128)(2,1)}, bf16[2,16,1024]{2,1,0:T(8,128)(2,1)S(1)}, u32[]{:S(2)}, u32[]{:S(2)}) collective-permute-start(bf16[2,16,1024]{2,1,0:T(8,128)(2,1)} %get-tuple-element.56), channel_id=1, source_target_pairs={{0,8},{1,9},{2,10},{3,11},{4,12},{5,13},{6,14},{7,15},{8,0},{9,1},... | collective-permute-start | bytes 196616 | tf_op jit(solution)/shard_map/ppermute | solution.py:386
  12.4 20.1 %collective-permute-start.4 = (bf16[2,16,1024]{2,1,0:T(8,128)(2,1)}, bf16[2,16,1024]{2,1,0:T(8,128)(2,1)S(1)}, u32[]{:S(2)}, u32[]{:S(2)}) collective-permute-start(bf16[2,16,1024]{2,1,0:T(8,128)(2,1)} %get-tuple-element.57), channel_id=1, source_target_pairs={{0,10},{1,11},{2,8},{3,9},{4,14},{5,15},{6,12},{7,13},{8,2},{9,3},... | collective-permute-start | bytes 196616 | tf_op jit(solution)/shard_map/ppermute | solution.py:386
  19.0 15.4 %collective-permute-start.5 = (bf16[2,16,1024]{2,1,0:T(8,128)(2,1)}, bf16[2,16,1024]{2,1,0:T(8,128)(2,1)S(1)}, u32[]{:S(2)}, u32[]{:S(2)}) collective-permute-start(bf16[2,16,1024]{2,1,0:T(8,128)(2,1)} %copy-done.19), channel_id=1, source_target_pairs={{0,12},{1,13},{2,14},{3,15},{4,8},{5,9},{6,10},{7,11},{8,4},{9,5},... | collective-permute-start | bytes 196616 | tf_op jit(solution)/shard_map/ppermute | solution.py:386
  22.6 14.2 %collective-permute-start.6 = (bf16[2,16,1024]{2,1,0:T(8,128)(2,1)}, bf16[2,16,1024]{2,1,0:T(8,128)(2,1)S(1)}, u32[]{:S(2)}, u32[]{:S(2)}) collective-permute-start(bf16[2,16,1024]{2,1,0:T(8,128)(2,1)} %copy-done.18), channel_id=1, source_target_pairs={{0,14},{1,15},{2,12},{3,13},{4,10},{5,11},{6,8},{7,9},{8,6},{9,7},... | collective-permute-start | bytes 196616 | tf_op jit(solution)/shard_map/ppermute | solution.py:386
  22.6 15.7 %collective-permute-start.14 = (bf16[3,16,1024]{2,1,0:T(8,128)(2,1)}, bf16[3,16,1024]{2,1,0:T(8,128)(2,1)S(1)}, u32[]{:S(2)}, u32[]{:S(2)}) collective-permute-start(bf16[3,16,1024]{2,1,0:T(8,128)(2,1)} %copy-done.17), channel_id=1, source_target_pairs={{0,2},{1,3},{2,0},{3,1},{4,6},{5,7},{6,4},{7,5},{8,10},{9,11},{10,... | collective-permute-start | bytes 294920 | tf_op jit(solution)/shard_map/ppermute | solution.py:386
  27.5 26.8 %copy-start.23 = (f32[128]{0:T(128)S(1)}, f32[128]{0:T(128)}, u32[]{:S(2)}) copy-start(f32[128]{0:T(128)} %param.19) | copy-start | bytes 1540
  32.4 10.5 %collective-permute-start.15 = (bf16[3,16,1024]{2,1,0:T(8,128)(2,1)S(1)}, bf16[3,16,1024]{2,1,0:T(8,128)(2,1)S(1)}, u32[]{:S(2)}, u32[]{:S(2)}) collective-permute-start(bf16[3,16,1024]{2,1,0:T(8,128)(2,1)S(1)} %copy-done.16), channel_id=1, source_target_pairs={{0,4},{1,5},{2,6},{3,7},{4,0},{5,1},{6,2},{7,3},{8,12},{9,13},{10,... | collective-permute-start | bytes 294920 | tf_op jit(solution)/shard_map/ppermute | solution.py:386
  32.5 10.5 %collective-permute-start.16 = (bf16[3,16,1024]{2,1,0:T(8,128)(2,1)S(1)}, bf16[3,16,1024]{2,1,0:T(8,128)(2,1)S(1)}, u32[]{:S(2)}, u32[]{:S(2)}) collective-permute-start(bf16[3,16,1024]{2,1,0:T(8,128)(2,1)S(1)} %copy-done.14), channel_id=1, source_target_pairs={{0,6},{1,7},{2,4},{3,5},{4,2},{5,3},{6,0},{7,1},{8,14},{9,15},{10,... | collective-permute-start | bytes 294920 | tf_op jit(solution)/shard_map/ppermute | solution.py:386
  34.4 12.3 %collective-permute-start.17 = (bf16[3,16,1024]{2,1,0:T(8,128)(2,1)S(1)}, bf16[3,16,1024]{2,1,0:T(8,128)(2,1)S(1)}, u32[]{:S(2)}, u32[]{:S(2)}) collective-permute-start(bf16[3,16,1024]{2,1,0:T(8,128)(2,1)S(1)} %copy-done.12), channel_id=1, source_target_pairs={{0,8},{1,9},{2,10},{3,11},{4,12},{5,13},{6,14},{7,15},{8,0},{9,1},... | collective-permute-start | bytes 294920 | tf_op jit(solution)/shard_map/ppermute | solution.py:386
  36.8 15.1 %collective-permute-start.18 = (bf16[3,16,1024]{2,1,0:T(8,128)(2,1)S(1)}, bf16[3,16,1024]{2,1,0:T(8,128)(2,1)S(1)}, u32[]{:S(2)}, u32[]{:S(2)}) collective-permute-start(bf16[3,16,1024]{2,1,0:T(8,128)(2,1)S(1)} %get-tuple-element.75), channel_id=1, source_target_pairs={{0,10},{1,11},{2,8},{3,9},{4,14},{5,15},{6,12},{7,13},{8,2},{9,3},... | collective-permute-start | bytes 294920 | tf_op jit(solution)/shard_map/ppermute | solution.py:386
  38.4 13.5 %collective-permute-start.19 = (bf16[3,16,1024]{2,1,0:T(8,128)(2,1)S(1)}, bf16[3,16,1024]{2,1,0:T(8,128)(2,1)S(1)}, u32[]{:S(2)}, u32[]{:S(2)}) collective-permute-start(bf16[3,16,1024]{2,1,0:T(8,128)(2,1)S(1)} %get-tuple-element.76), channel_id=1, source_target_pairs={{0,12},{1,13},{2,14},{3,15},{4,8},{5,9},{6,10},{7,11},{8,4},{9,5},... | collective-permute-start | bytes 294920 | tf_op jit(solution)/shard_map/ppermute | solution.py:386
  42.9 11.5 %collective-permute-start.20 = (bf16[3,16,1024]{2,1,0:T(8,128)(2,1)S(1)}, bf16[3,16,1024]{2,1,0:T(8,128)(2,1)S(1)}, u32[]{:S(2)}, u32[]{:S(2)}) collective-permute-start(bf16[3,16,1024]{2,1,0:T(8,128)(2,1)S(1)} %get-tuple-element.77), channel_id=1, source_target_pairs={{0,14},{1,15},{2,12},{3,13},{4,10},{5,11},{6,8},{7,9},{8,6},{9,7},... | collective-permute-start | bytes 294920 | tf_op jit(solution)/shard_map/ppermute | solution.py:386
  43.0 14.5 %collective-permute-start.7 = (bf16[2,16,1024]{2,1,0:T(8,128)(2,1)}, bf16[2,16,1024]{2,1,0:T(8,128)(2,1)S(1)}, u32[]{:S(2)}, u32[]{:S(2)}) collective-permute-start(bf16[2,16,1024]{2,1,0:T(8,128)(2,1)} %get-tuple-element.61), channel_id=1, source_target_pairs={{0,2},{1,3},{2,0},{3,1},{4,6},{5,7},{6,4},{7,5},{8,10},{9,11},{10,... | collective-permute-start | bytes 196616 | tf_op jit(solution)/shard_map/ppermute | solution.py:386
  46.7 12.0 %collective-permute-start.8 = (bf16[2,16,1024]{2,1,0:T(8,128)(2,1)}, bf16[2,16,1024]{2,1,0:T(8,128)(2,1)S(1)}, u32[]{:S(2)}, u32[]{:S(2)}) collective-permute-start(bf16[2,16,1024]{2,1,0:T(8,128)(2,1)} %get-tuple-element.62), channel_id=1, source_target_pairs={{0,4},{1,5},{2,6},{3,7},{4,0},{5,1},{6,2},{7,3},{8,12},{9,13},{10,... | collective-permute-start | bytes 196616 | tf_op jit(solution)/shard_map/ppermute | solution.py:386
  51.8 10.6 %collective-permute-start.9 = (bf16[2,16,1024]{2,1,0:T(8,128)(2,1)}, bf16[2,16,1024]{2,1,0:T(8,128)(2,1)S(1)}, u32[]{:S(2)}, u32[]{:S(2)}) collective-permute-start(bf16[2,16,1024]{2,1,0:T(8,128)(2,1)} %get-tuple-element.63), channel_id=1, source_target_pairs={{0,6},{1,7},{2,4},{3,5},{4,2},{5,3},{6,0},{7,1},{8,14},{9,15},{10,... | collective-permute-start | bytes 196616 | tf_op jit(solution)/shard_map/ppermute | solution.py:386
  51.8 11.1 %collective-permute-start.10 = (bf16[2,16,1024]{2,1,0:T(8,128)(2,1)}, bf16[2,16,1024]{2,1,0:T(8,128)(2,1)S(1)}, u32[]{:S(2)}, u32[]{:S(2)}) collective-permute-start(bf16[2,16,1024]{2,1,0:T(8,128)(2,1)} %get-tuple-element.64), channel_id=1, source_target_pairs={{0,8},{1,9},{2,10},{3,11},{4,12},{5,13},{6,14},{7,15},{8,0},{9,1},... | collective-permute-start | bytes 196616 | tf_op jit(solution)/shard_map/ppermute | solution.py:386
  54.4 8.6 %collective-permute-start.11 = (bf16[2,16,1024]{2,1,0:T(8,128)(2,1)S(1)}, bf16[2,16,1024]{2,1,0:T(8,128)(2,1)S(1)}, u32[]{:S(2)}, u32[]{:S(2)}) collective-permute-start(bf16[2,16,1024]{2,1,0:T(8,128)(2,1)S(1)} %get-tuple-element.65), channel_id=1, source_target_pairs={{0,10},{1,11},{2,8},{3,9},{4,14},{5,15},{6,12},{7,13},{8,2},{9,3},... | collective-permute-start | bytes 196616 | tf_op jit(solution)/shard_map/ppermute | solution.py:386
  57.5 8.4 %collective-permute-start.12 = (bf16[2,16,1024]{2,1,0:T(8,128)(2,1)S(1)}, bf16[2,16,1024]{2,1,0:T(8,128)(2,1)S(1)}, u32[]{:S(2)}, u32[]{:S(2)}) collective-permute-start(bf16[2,16,1024]{2,1,0:T(8,128)(2,1)S(1)} %get-tuple-element.66), channel_id=1, source_target_pairs={{0,12},{1,13},{2,14},{3,15},{4,8},{5,9},{6,10},{7,11},{8,4},{9,5},... | collective-permute-start | bytes 196616 | tf_op jit(solution)/shard_map/ppermute | solution.py:386
  58.7 8.1 %collective-permute-start.13 = (bf16[2,16,1024]{2,1,0:T(8,128)(2,1)S(1)}, bf16[2,16,1024]{2,1,0:T(8,128)(2,1)S(1)}, u32[]{:S(2)}, u32[]{:S(2)}) collective-permute-start(bf16[2,16,1024]{2,1,0:T(8,128)(2,1)S(1)} %get-tuple-element.67), channel_id=1, source_target_pairs={{0,14},{1,15},{2,12},{3,13},{4,10},{5,11},{6,8},{7,9},{8,6},{9,7},... | collective-permute-start | bytes 196616 | tf_op jit(solution)/shard_map/ppermute | solution.py:386
  62.4 9.1 %collective-permute-start.21 = (bf16[3,16,1024]{2,1,0:T(8,128)(2,1)S(1)}, bf16[3,16,1024]{2,1,0:T(8,128)(2,1)S(1)}, u32[]{:S(2)}, u32[]{:S(2)}) collective-permute-start(bf16[3,16,1024]{2,1,0:T(8,128)(2,1)S(1)} %get-tuple-element.79), channel_id=1, source_target_pairs={{0,2},{1,3},{2,0},{3,1},{4,6},{5,7},{6,4},{7,5},{8,10},{9,11},{10,... | collective-permute-start | bytes 294920 | tf_op jit(solution)/shard_map/ppermute | solution.py:386
  62.9 8.6 %collective-permute-start.22 = (bf16[3,16,1024]{2,1,0:T(8,128)(2,1)S(1)}, bf16[3,16,1024]{2,1,0:T(8,128)(2,1)S(1)}, u32[]{:S(2)}, u32[]{:S(2)}) collective-permute-start(bf16[3,16,1024]{2,1,0:T(8,128)(2,1)S(1)} %get-tuple-element.80), channel_id=1, source_target_pairs={{0,4},{1,5},{2,6},{3,7},{4,0},{5,1},{6,2},{7,3},{8,12},{9,13},{10,... | collective-permute-start | bytes 294920 | tf_op jit(solution)/shard_map/ppermute | solution.py:386
  63.0 13.3 %collective-permute-start.23 = (bf16[3,16,1024]{2,1,0:T(8,128)(2,1)S(1)}, bf16[3,16,1024]{2,1,0:T(8,128)(2,1)S(1)}, u32[]{:S(2)}, u32[]{:S(2)}) collective-permute-start(bf16[3,16,1024]{2,1,0:T(8,128)(2,1)S(1)} %get-tuple-element.81), channel_id=1, source_target_pairs={{0,6},{1,7},{2,4},{3,5},{4,2},{5,3},{6,0},{7,1},{8,14},{9,15},{10,... | collective-permute-start | bytes 294920 | tf_op jit(solution)/shard_map/ppermute | solution.py:386
  65.9 10.4 %collective-permute-start.24 = (bf16[3,16,1024]{2,1,0:T(8,128)(2,1)S(1)}, bf16[3,16,1024]{2,1,0:T(8,128)(2,1)S(1)}, u32[]{:S(2)}, u32[]{:S(2)}) collective-permute-start(bf16[3,16,1024]{2,1,0:T(8,128)(2,1)S(1)} %get-tuple-element.82), channel_id=1, source_target_pairs={{0,8},{1,9},{2,10},{3,11},{4,12},{5,13},{6,14},{7,15},{8,0},{9,1},... | collective-permute-start | bytes 294920 | tf_op jit(solution)/shard_map/ppermute | solution.py:386
  66.8 14.0 %collective-permute-start.25 = (bf16[3,16,1024]{2,1,0:T(8,128)(2,1)S(1)}, bf16[3,16,1024]{2,1,0:T(8,128)(2,1)S(1)}, u32[]{:S(2)}, u32[]{:S(2)}) collective-permute-start(bf16[3,16,1024]{2,1,0:T(8,128)(2,1)S(1)} %get-tuple-element.83), channel_id=1, source_target_pairs={{0,10},{1,11},{2,8},{3,9},{4,14},{5,15},{6,12},{7,13},{8,2},{9,3},... | collective-permute-start | bytes 294920 | tf_op jit(solution)/shard_map/ppermute | solution.py:386
  71.4 9.4 %collective-permute-start.26 = (bf16[3,16,1024]{2,1,0:T(8,128)(2,1)S(1)}, bf16[3,16,1024]{2,1,0:T(8,128)(2,1)S(1)}, u32[]{:S(2)}, u32[]{:S(2)}) collective-permute-start(bf16[3,16,1024]{2,1,0:T(8,128)(2,1)S(1)} %get-tuple-element.84), channel_id=1, source_target_pairs={{0,12},{1,13},{2,14},{3,15},{4,8},{5,9},{6,10},{7,11},{8,4},{9,5},... | collective-permute-start | bytes 294920 | tf_op jit(solution)/shard_map/ppermute | solution.py:386
  71.5 9.4 %collective-permute-start.27 = (bf16[3,16,1024]{2,1,0:T(8,128)(2,1)S(1)}, bf16[3,16,1024]{2,1,0:T(8,128)(2,1)S(1)}, u32[]{:S(2)}, u32[]{:S(2)}) collective-permute-start(bf16[3,16,1024]{2,1,0:T(8,128)(2,1)S(1)} %get-tuple-element.85), channel_id=1, source_target_pairs={{0,14},{1,15},{2,12},{3,13},{4,10},{5,11},{6,8},{7,9},{8,6},{9,7},... | collective-permute-start | bytes 294920 | tf_op jit(solution)/shard_map/ppermute | solution.py:386
  76.3 11.0 %collective-permute-start.28 = (bf16[5,2,1,1024]{3,2,1,0:T(2,128)(2,1)S(1)}, bf16[5,2,1,1024]{3,2,1,0:T(2,128)(2,1)S(1)}, u32[]{:S(2)}, u32[]{:S(2)}) collective-permute-start(bf16[5,2,1,1024]{3,2,1,0:T(2,128)(2,1)S(1)} %copy-done.21), channel_id=1, source_target_pairs={{15,0},{2,1},{1,2},{4,3},{3,4},{6,5},{5,6},{8,7},{7,8},{10,9},{9,1... | collective-permute-start | bytes 61448 | tf_op jit(solution)/shard_map/ppermute | solution.py:396
  76.4 10.9 %collective-permute-start.30 = (bf16[2,2,2,1024]{3,2,1,0:T(2,128)(2,1)S(1)}, bf16[2,2,2,1024]{3,2,1,0:T(2,128)(2,1)S(1)}, u32[]{:S(2)}, u32[]{:S(2)}) collective-permute-start(bf16[2,2,2,1024]{3,2,1,0:T(2,128)(2,1)S(1)} %get-tuple-element.98), channel_id=1, source_target_pairs={{15,0},{2,1},{1,2},{4,3},{3,4},{6,5},{5,6},{8,7},{7,8},{10,9},{9,1... | collective-permute-start | bytes 49160 | tf_op jit(solution)/shard_map/ppermute | solution.py:396
  81.5 6.0 %collective-permute-start.29 = (bf16[3,2,2,1024]{3,2,1,0:T(2,128)(2,1)S(1)}, bf16[3,2,2,1024]{3,2,1,0:T(2,128)(2,1)S(1)}, u32[]{:S(2)}, u32[]{:S(2)}) collective-permute-start(bf16[3,2,2,1024]{3,2,1,0:T(2,128)(2,1)S(1)} %get-tuple-element.95), channel_id=1, source_target_pairs={{15,0},{2,1},{1,2},{4,3},{3,4},{6,5},{5,6},{8,7},{7,8},{10,9},{9,1... | collective-permute-start | bytes 73736 | tf_op jit(solution)/shard_map/ppermute | solution.py:396
  (23 other events, 158.9 us)
